TPU v7x, 32 devices: a whole 2x2x4 slice. The times are simulated.
32 devices in a mesh: row: 4 (over z), col: 4 (over x, core), depth: 2 (over y).
Axes of the slice: x: 2, y: 2, z: 4, core: 2. Of those that a mesh axis runs over, the one named last changes fastest.
Arguments:
- tokens: bfloat16 [128, 12288], P('depth', 'row'), may hold values from -6 to 6
- w_in: bfloat16 [12288, 24576], P('row', ('col', 'depth')), may hold values from -0.0546875 to 0.0546875
- w_out: bfloat16 [24576, 12288], P(('col', 'depth'), 'row'), may hold values from -0.0390625 to 0.0390625
- cotangent: bfloat16 [128, 12288], P('depth', 'row'), may hold values from -6 to 6
Outputs:
- output: bfloat16 [128, 12288], P(('col', 'depth'), 'row')
- grad_input: bfloat16 [128, 12288], P(('col', 'depth'), 'row')
- grad_w_in: bfloat16 [12288, 24576], P('row', ('col', 'depth'))
- grad_w_out: bfloat16 [24576, 12288], P(('col', 'depth'), 'row')
All inputs are finite; a program needn't handle non-finite values.
Results may differ from a plain program's by a relative error of at most 0.019.
Values may be sent and summed in bfloat16 or wider, within the bound.
A program may use at most 192 MiB of HBM per device.

v0:
```python
import math

import jax
import jax.numpy as jnp
from jax import lax
from jax.sharding import PartitionSpec as P

gelu_coef = math.sqrt(2.0 / math.pi)


def gelu_parts(preact):
    inner = gelu_coef * (preact + 0.044715 * preact * preact * preact)
    tanh_val = jnp.tanh(inner)
    gelu_value = 0.5 * preact * (1.0 + tanh_val)
    gelu_slope = 0.5 * (1.0 + tanh_val) + 0.5 * preact * (1.0 - tanh_val * tanh_val) * gelu_coef * (
        1.0 + 3.0 * 0.044715 * preact * preact
    )
    return (gelu_value, gelu_slope)


def contract_rows(left, right):
    return lax.dot_general(
        left, right, (((0,), (0,)), ((), ())), preferred_element_type=jnp.float32
    )


def contract_cols(left, right):
    return lax.dot_general(
        left, right, (((1,), (1,)), ((), ())), preferred_element_type=jnp.float32
    )


def body(tokens, w_in, w_out, cotangent):
    all_tokens, all_grads = (
        lax.all_gather(tokens, "depth", axis=0, tiled=True),
        lax.all_gather(cotangent, "depth", axis=0, tiled=True),
    )
    tok_rows = all_tokens.shape[0]
    grad_scale = tok_rows ** (-0.5)
    preact = lax.psum_scatter(
        jnp.dot(all_tokens, w_in, preferred_element_type=jnp.float32).astype(jnp.bfloat16),
        "row",
        scatter_dimension=0,
        tiled=True,
    ).astype(jnp.float32)
    gelu_value, gelu_slope = gelu_parts(preact)
    block = lax.all_gather(gelu_value.astype(jnp.bfloat16), "row", axis=0, tiled=True)
    product = jnp.dot(block, w_out, preferred_element_type=jnp.float32)
    out_total = product
    down_part = contract_rows(block, all_grads)
    act_grad = lax.psum_scatter(
        contract_cols(all_grads, w_out).astype(jnp.bfloat16), "row", scatter_dimension=0, tiled=True
    ).astype(jnp.float32)
    hidden_share = (act_grad * gelu_slope).astype(jnp.bfloat16)
    block = lax.all_gather(hidden_share, "row", axis=0, tiled=True)
    product = contract_cols(block, w_in)
    up_part = contract_rows(all_tokens, block)
    output = lax.psum_scatter(
        out_total.astype(jnp.bfloat16), ("col", "depth"), scatter_dimension=0, tiled=True
    )
    grad_input = lax.psum_scatter(
        product.astype(jnp.bfloat16), ("col", "depth"), scatter_dimension=0, tiled=True
    )
    grad_w_in = (up_part * grad_scale).astype(jnp.bfloat16)
    grad_w_out = (down_part * grad_scale).astype(jnp.bfloat16)
    return (output, grad_input, grad_w_in, grad_w_out)


def solution(mesh):
    in_specs = (
        P("depth", "row"),
        P("row", ("col", "depth")),
        P(("col", "depth"), "row"),
        P("depth", "row"),
    )
    out_specs = (
        P(("col", "depth"), "row"),
        P(("col", "depth"), "row"),
        P("row", ("col", "depth")),
        P(("col", "depth"), "row"),
    )
    return jax.shard_map(body, mesh=mesh, in_specs=in_specs, out_specs=out_specs, check_vma=False)
```

profile of v0, /device:TPU:0, one launch (start us, length us, event | category | flops | bytes accessed | tf_op | source)
XLA Modules:
  0.0 195.0 jit_solution(775299425980377137)
XLA Ops:
  7.2 0.0 copy-start
  7.2 0.0 reduce-scatter.9.cloned.1.call-start
  7.2 13.1 %all_gather.14 = bf16[128,3072]{1,0:T(8,128)(2,1)S(1)} all-gather(bf16[64,3072]{1,0:T(8,128)(2,1)} %param.7), channel_id=1, replica_groups=mesh['row'=4,'col'=4,'depth'=2] {'depth'}, dimensions={0}, use_global_device_ids=true | all-gather | bytes 1179648 | tf_op jit(solution)/shard_map/all_gather | solution.py:36
  20.4 13.6 %convolution_convert_fusion.1 = bf16[128,3072]{1,0:T(8,128)(2,1)} fusion(bf16[128,3072]{1,0:T(8,128)(2,1)S(1)} %all_gather.14, bf16[3072,3072]{1,0:T(8,128)(2,1)} %param.6), kind=kOutput, calls=%fused_computation.4 | convolution fusion | flops 2416312320 | bytes 20447232 | tf_op jit(solution)/shard_map/dot_general | solution.py:28
  33.9 0.0 reduce-scatter.9.cloned.1.call-update
  33.9 0.0 reduce-scatter.5.cloned.1.call-start
  34.0 0.0 copy-done
  34.0 11.0 %all_gather.12 = bf16[128,3072]{1,0:T(8,128)(2,1)S(1)} all-gather(bf16[64,3072]{1,0:T(8,128)(2,1)S(1)} %copy-done), channel_id=1, replica_groups=mesh['row'=4,'col'=4,'depth'=2] {'depth'}, dimensions={0}, use_global_device_ids=true | all-gather | bytes 1179648 | tf_op jit(solution)/shard_map/all_gather | solution.py:35
  45.0 10.0 %convolution_convert_fusion.3 = bf16[128,3072]{1,0:T(8,128)(2,1)} fusion(bf16[128,3072]{1,0:T(8,128)(2,1)S(1)} %all_gather.12, bf16[3072,3072]{1,0:T(8,128)(2,1)} %param.5), kind=kOutput, calls=%fused_computation.6 | convolution fusion | flops 2416312320 | bytes 20447232 | tf_op jit(solution)/shard_map/dot_general | solution.py:41
  54.9 0.0 reduce-scatter.5.cloned.1.call-update
  55.0 0.0 reduce-scatter.7.cloned.1.call-start
  55.0 3.8 %reduce-scatter.9.cloned.1.call-done = bf16[32,3072]{1,0:T(8,128)(2,1)} async-done(((bf16[128,3072]{1,0:T(8,128)(2,1)}), bf16[32,3072]{1,0:T(8,128)(2,1)}) %reduce-scatter.9.cloned.1.call-update) | async-done | bytes 196624 | tf_op jit(solution)/shard_map/reduce_scatter | solution.py:51
  58.8 25.5 %reduce-scatter.5.cloned.1.call-done = bf16[32,3072]{1,0:T(8,128)(2,1)} async-done(((bf16[128,3072]{1,0:T(8,128)(2,1)}), bf16[32,3072]{1,0:T(8,128)(2,1)}) %reduce-scatter.5.cloned.1.call-update) | async-done | bytes 196624 | tf_op jit(solution)/shard_map/reduce_scatter | solution.py:40
  84.3 1.3 fusion.8
  85.6 18.0 %all_gather.13 = bf16[128,3072]{1,0:T(8,128)(2,1)S(1)} all-gather(bf16[32,3072]{1,0:T(8,128)(2,1)S(1)} %get-tuple-element.9), channel_id=1, replica_groups=mesh['row'=4,'col'=4,'depth'=2] {'row'}, dimensions={0}, use_global_device_ids=true | all-gather | bytes 983040 | tf_op jit(solution)/shard_map/all_gather | solution.py:47
  103.6 9.9 %convolution_convert_fusion.2 = bf16[128,3072]{1,0:T(8,128)(2,1)} fusion(bf16[128,3072]{1,0:T(8,128)(2,1)S(1)} %all_gather.13, bf16[3072,3072]{1,0:T(8,128)(2,1)} %param.6), kind=kOutput, calls=%fused_computation.5 | convolution fusion | flops 2416312320 | bytes 20447232 | tf_op jit(solution)/shard_map/dot_general | solution.py:48
  113.5 0.0 reduce-scatter.7.cloned.1.call-update
  113.5 0.0 reduce-scatter.11.cloned.1.call-start
  113.6 17.5 %all_gather.15 = bf16[128,3072]{1,0:T(8,128)(2,1)S(1)} all-gather(bf16[32,3072]{1,0:T(8,128)(2,1)S(1)} %get-tuple-element.8), channel_id=1, replica_groups=mesh['row'=4,'col'=4,'depth'=2] {'row'}, dimensions={0}, use_global_device_ids=true | all-gather | bytes 983040 | tf_op jit(solution)/shard_map/all_gather | solution.py:55
  131.1 13.7 %convolution_convert_fusion = bf16[128,3072]{1,0:T(8,128)(2,1)} fusion(bf16[128,3072]{1,0:T(8,128)(2,1)S(1)} %all_gather.15, bf16[3072,3072]{1,0:T(8,128)(2,1)} %param.5), kind=kOutput, calls=%fused_computation.3 | convolution fusion | flops 2416312320 | bytes 20447232 | tf_op jit(solution)/shard_map/dot_general | solution.py:28
  144.8 0.0 reduce-scatter.11.cloned.1.call-update
  144.8 9.5 %fusion = bf16[3072,3072]{0,1:T(8,128)(2,1)} fusion(bf16[128,3072]{1,0:T(8,128)(2,1)S(1)} %all_gather.15, bf16[128,3072]{1,0:T(8,128)(2,1)S(1)} %all_gather.12), kind=kOutput, calls=%fused_computation.2 | convolution fusion | flops 2434793472 | bytes 20447232 | tf_op jit(solution)/shard_map/dot_general | solution.py:22
  154.4 24.6 %copy.8 = bf16[3072,3072]{1,0:T(8,128)(2,1)} copy(bf16[3072,3072]{0,1:T(8,128)(2,1)} %fusion) | data formatting | bytes 37748736
  179.0 9.5 %multiply_convert_fusion = bf16[3072,3072]{1,0:T(8,128)(2,1)} fusion(bf16[128,3072]{1,0:T(8,128)(2,1)S(1)} %all_gather.13, bf16[128,3072]{1,0:T(8,128)(2,1)S(1)} %all_gather.14), kind=kOutput, calls=%fused_computation | convolution fusion | flops 2434793472 | bytes 20447232 | tf_op jit(solution)/shard_map/dot_general | solution.py:22
  188.5 0.0 reduce-scatter.7.cloned.1.call-done
  188.5 0.0 reduce-scatter.11.cloned.1.call-done
Async XLA Ops:
  7.2 26.8 %copy-start = (bf16[64,3072]{1,0:T(8,128)(2,1)S(1)}, bf16[64,3072]{1,0:T(8,128)(2,1)}, u32[]{:S(2)}) copy-start(bf16[64,3072]{1,0:T(8,128)(2,1)} %param.4) | copy-start | bytes 1179652
  7.2 51.6 %reduce-scatter.9.cloned.1.call-start = ((), (), s32[]{:S(2)}) async-start(), calls=%async_computation.6 | async-start | bytes 983040 | tf_op jit(solution)/shard_map/reduce_scatter | solution.py:51
  33.9 50.4 %reduce-scatter.5.cloned.1.call-start = ((), (), s32[]{:S(2)}) async-start(), calls=%async_computation.4 | async-start | bytes 983040 | tf_op jit(solution)/shard_map/reduce_scatter | solution.py:40
  55.0 133.5 %reduce-scatter.7.cloned.1.call-start = ((), (), s32[]{:S(2)}) async-start(), calls=%async_computation.5 | async-start | bytes 884736 | tf_op jit(solution)/shard_map/reduce_scatter | solution.py:58
  113.5 75.0 %reduce-scatter.11.cloned.1.call-start = ((), (), s32[]{:S(2)}) async-start(), calls=%async_computation.7 | async-start | bytes 884736 | tf_op jit(solution)/shard_map/reduce_scatter | solution.py:61
Sparse Core Ops, SparseCore 0:
  34.1 24.7 reduce-scatter.8
  61.7 22.5 reduce-scatter.4
  113.6 34.2 reduce-scatter.6
  151.5 35.0 reduce-scatter.10
where the time goes:
time: 196 us; the launch traced here: 195 us
  matrix products  66.1 us (34%)
  blocking collectives  59.7 us (30%)
  waiting for transfers between devices  29.3 us (15%)
  local copies, waits for them, and re-layouts  24.7 us (13%)
  between operations  13.8 us (7%)
    dot_general x2, matrix products, contract_cols(): lax.dot_general(left, right, (((1,), (1,)), ((), ())), preferred_element_...  27.3 us
    reduce_scatter x1, waiting for transfers between devices, body(): lax.psum_scatter(jnp.dot(all_tokens, w_in, preferred_element_type=jnp.flo...  25.5 us
    unnamed x3, local copies, waits for them, and re-layouts  24.7 us
    dot_general x2, matrix products, contract_rows(): lax.dot_general(left, right, (((0,), (0,)), ((), ())), preferred_element_...  19 us
    all_gather x1, blocking collectives, body(): lax.all_gather(gelu_value.astype(jnp.bfloat16), 'row', axis=0, tiled=True)  18 us
    all_gather x1, blocking collectives, body(): block = lax.all_gather(hidden_share, 'row', axis=0, tiled=True)  17.5 us
    all_gather x1, blocking collectives, body(): lax.all_gather(cotangent, 'depth', axis=0, tiled=True)  13.1 us
    all_gather x1, blocking collectives, body(): lax.all_gather(tokens, 'depth', axis=0, tiled=True)  11 us
  transfers between devices with their start and end apart: 4, of which 2 were waited for; matrix products, arithmetic and copies ran while one was open for 35% of the time, Pallas kernels for 0%

commit v1 on v0

v1 whole, which is shorter than its diff:
```python
import functools
import math

import jax
import jax.numpy as jnp
from jax import lax
from jax.experimental import pallas as pl
from jax.experimental.pallas import tpu as pltpu
from jax.sharding import PartitionSpec as P

MESH = pl.DeviceIdType.MESH
CHUNK = 256
TILE = 768
HOP = 2

gelu_coef = math.sqrt(2.0 / math.pi)


def gelu_parts(preact):
    inner = gelu_coef * (preact + 0.044715 * preact * preact * preact)
    tanh_val = jnp.tanh(inner)
    gelu_value = 0.5 * preact * (1.0 + tanh_val)
    gelu_slope = 0.5 * (1.0 + tanh_val) + 0.5 * preact * (1.0 - tanh_val * tanh_val) * gelu_coef * (
        1.0 + 3.0 * 0.044715 * preact * preact
    )
    return (gelu_value, gelu_slope)


def contract_rows(left, right):
    return lax.dot_general(
        left, right, (((0,), (0,)), ((), ())), preferred_element_type=jnp.float32
    )


def contract_cols(left, right):
    return lax.dot_general(
        left, right, (((1,), (1,)), ((), ())), preferred_element_type=jnp.float32
    )


def kernel(
    n_row,
    n_col,
    n_depth,
    tok_ref,
    w_in_ref,
    w_out_ref,
    cot_ref,
    out_ref,
    gin_ref,
    tok_out,
    cot_out,
    act_out,
    hid_out,
    w_in_v,
    w_out_v,
    tok_all,
    cot_all,
    own,
    from_left,
    from_right,
    to_right,
    to_left,
    total,
    slope,
    act_all,
    hid_all,
    acc_out,
    acc_gin,
    pair_send,
    pair_recv,
    part_send,
    part_recv,
    w_in_sem,
    w_out_sem,
    keep_sem,
    left_sems,
    right_sems,
    depth_sems,
    swap_sems,
    pair_sems,
    part_sems,
):
    row = lax.axis_index("row")
    col = lax.axis_index("col")
    depth = lax.axis_index("depth")
    side = lax.rem(col, 2)
    half_col = col // 2
    mate = col + 1 - 2 * side
    slice_rows = tok_ref.shape[0]
    half_rows = slice_rows // 2
    ff = w_in_ref.shape[1]
    d_model = w_in_ref.shape[0]
    steps = ff // CHUNK
    msgs = 2 * steps
    group = (n_col // 2) * n_depth
    me = half_col * n_depth + depth
    block_rows = acc_out.shape[0] // n_col
    piece_rows = block_rows // n_depth
    last_row = n_row - 1

    def cols(j):
        return pl.ds(pl.multiple_of(j * CHUNK, CHUNK), CHUNK)

    def w_in_copy(j):
        return pltpu.make_async_copy(w_in_ref.at[:, cols(j)], w_in_v.at[j], w_in_sem.at[j])

    def w_out_copy(j):
        return pltpu.make_async_copy(w_out_ref.at[cols(j), :], w_out_v.at[j], w_out_sem.at[j])

    @pl.loop(0, steps)
    def _(j):
        w_in_copy(j).start()

    def place(index):
        return {"col": 2 * (index // n_depth) + side, "depth": lax.rem(index, n_depth)}

    barrier = pltpu.get_barrier_semaphore()

    @pl.when(row > 0)
    def _():
        pl.semaphore_signal(barrier, inc=1, device_id={"row": row - 1}, device_id_type=MESH)

    @pl.when(row < last_row)
    def _():
        pl.semaphore_signal(barrier, inc=1, device_id={"row": row + 1}, device_id_type=MESH)

    pl.semaphore_signal(barrier, inc=1, device_id={"col": mate}, device_id_type=MESH)
    for k in range(1, group):
        pl.semaphore_signal(
            barrier, inc=1, device_id=place(lax.rem(me + k, group)), device_id_type=MESH
        )
    own_rows = pl.ds(pl.multiple_of(depth * slice_rows, slice_rows), slice_rows)
    tok_all[own_rows, :] = tok_ref[...]
    cot_all[own_rows, :] = cot_ref[...]
    acc_out[...] = jnp.zeros_like(acc_out)
    acc_gin[...] = jnp.zeros_like(acc_gin)

    edges = jnp.where(row > 0, 1, 0) + jnp.where(row < last_row, 1, 0)
    pl.semaphore_wait(barrier, group + edges)

    def depth_copy(a, k):
        src, dst = ((tok_ref, tok_all), (cot_ref, cot_all))[a]
        here = pl.multiple_of(side * half_rows, half_rows)
        there = pl.multiple_of(depth * slice_rows + side * half_rows, half_rows)
        return pltpu.make_async_remote_copy(
            src_ref=src.at[pl.ds(here, half_rows), :],
            dst_ref=dst.at[pl.ds(there, half_rows), :],
            send_sem=depth_sems.at[0, a, k - 1],
            recv_sem=depth_sems.at[1, a, k - 1],
            device_id={"depth": lax.rem(depth + k, n_depth)},
            device_id_type=MESH,
        )

    def swap_copy(a, k):
        dst = (tok_all, cot_all)[a]
        origin = lax.rem(depth + n_depth - k, n_depth)
        rows = pl.ds(pl.multiple_of(origin * slice_rows + side * half_rows, half_rows), half_rows)
        return pltpu.make_async_remote_copy(
            src_ref=dst.at[rows, :],
            dst_ref=dst.at[rows, :],
            send_sem=swap_sems.at[0, a, k - 1],
            recv_sem=swap_sems.at[1, a, k - 1],
            device_id={"col": mate},
            device_id_type=MESH,
        )

    for a in range(2):
        for k in range(1, n_depth):
            depth_copy(a, k).start()

    def pass_on(a):
        for k in range(1, n_depth):
            depth_copy(a, k).wait_recv()
            swap_copy(a, k).start()

    def arrived(a):
        for k in range(1, n_depth):
            swap_copy(a, k).wait_recv()

    def right_copy(m):
        return pltpu.make_async_remote_copy(
            src_ref=to_right.at[m],
            dst_ref=from_left.at[m],
            send_sem=left_sems.at[0, m],
            recv_sem=left_sems.at[1, m],
            device_id={"row": lax.rem(row + 1, n_row)},
            device_id_type=MESH,
        )

    def left_copy(m):
        return pltpu.make_async_remote_copy(
            src_ref=to_left.at[m],
            dst_ref=from_right.at[m],
            send_sem=right_sems.at[0, m],
            recv_sem=right_sems.at[1, m],
            device_id={"row": lax.rem(row + n_row - 1, n_row)},
            device_id_type=MESH,
        )

    def pair_copy(a, i):
        return pltpu.make_async_remote_copy(
            src_ref=pair_send.at[a, i],
            dst_ref=pair_recv.at[a, i],
            send_sem=pair_sems.at[0, a, i],
            recv_sem=pair_sems.at[1, a, i],
            device_id={"col": mate},
            device_id_type=MESH,
        )

    def part_copy(a, k):
        return pltpu.make_async_remote_copy(
            src_ref=part_send.at[a, lax.rem(me + k, group)],
            dst_ref=part_recv.at[a, k - 1],
            send_sem=part_sems.at[0, a, k - 1],
            recv_sem=part_sems.at[1, a, k - 1],
            device_id=place(lax.rem(me + k, group)),
            device_id_type=MESH,
        )

    def send_pair(a, acc):
        for i in range(n_col // 2):
            rows = pl.ds(pl.multiple_of((2 * i + 1 - side) * block_rows, block_rows), block_rows)
            pair_send[a, i] = acc[rows, :].astype(jnp.bfloat16)
            pair_copy(a, i).start()

    def send_parts(a, acc):
        for i in range(n_col // 2):
            pair_copy(a, i).wait_recv()
            for p in range(n_depth):
                rows = pl.ds(
                    pl.multiple_of((2 * i + side) * block_rows + p * piece_rows, piece_rows),
                    piece_rows,
                )
                part_send[a, i * n_depth + p] = (
                    acc[rows, :]
                    + pair_recv[a, i, p * piece_rows : (p + 1) * piece_rows, :].astype(jnp.float32)
                ).astype(jnp.bfloat16)
        for k in range(1, group):
            part_copy(a, k).start()

    def finish(a, ref):
        result = part_send[a, me].astype(jnp.float32)
        for k in range(1, group):
            part_copy(a, k).wait_recv()
            result = result + part_recv[a, k - 1].astype(jnp.float32)
        ref[...] = result.astype(ref.dtype)

    outs = ((tok_all, tok_out), (cot_all, cot_out), (act_all, act_out), (hid_all, hid_out))

    def keep(a):
        return pltpu.make_async_copy(outs[a][0], outs[a][1], keep_sem.at[a])

    pass_on(0)
    arrived(0)
    keep(0).start()

    far = jnp.maximum(row, last_row - row)
    wait_lag = min(steps, HOP * (n_row // 2))

    @pl.loop(0, msgs + HOP * last_row)
    def _(t):
        @pl.when(t < steps)
        def _():
            w_out_copy(t).start()
            w_in_copy(t).wait()
            own[t] = jnp.dot(
                tok_all[...], w_in_v[t], preferred_element_type=jnp.float32
            ).astype(jnp.bfloat16)

        ready = t - wait_lag

        @pl.when(jnp.logical_and(ready >= 0, ready < steps))
        def _():
            w_out_copy(ready).wait()

        @pl.when(t == min(4, steps - 1))
        def _():
            pass_on(1)

        @pl.when(t == steps)
        def _():
            arrived(1)
            keep(1).start()

        @pl.when(jnp.logical_and(t >= steps, t < msgs))
        def _():
            own[t] = contract_cols(cot_all[...], w_out_v[t - steps]).astype(jnp.bfloat16)

        m1 = t - HOP * row

        @pl.when(jnp.logical_and(m1 >= 0, m1 < msgs))
        def _():
            @pl.when(row == 0)
            def _():
                to_right[m1] = own[m1]

            @pl.when(row > 0)
            def _():
                right_copy(m1).wait_recv()

                @pl.when(row < last_row)
                def _():
                    to_right[m1] = (
                        own[m1].astype(jnp.float32) + from_left[m1].astype(jnp.float32)
                    ).astype(jnp.bfloat16)

            @pl.when(row < last_row)
            def _():
                right_copy(m1).start()

        m2 = t - HOP * (last_row - row)

        @pl.when(jnp.logical_and(m2 >= 0, m2 < msgs))
        def _():
            @pl.when(row == last_row)
            def _():
                to_left[m2] = own[m2]

            @pl.when(row < last_row)
            def _():
                left_copy(m2).wait_recv()

                @pl.when(row > 0)
                def _():
                    to_left[m2] = (
                        own[m2].astype(jnp.float32) + from_right[m2].astype(jnp.float32)
                    ).astype(jnp.bfloat16)

            @pl.when(row > 0)
            def _():
                left_copy(m2).start()

        m = t - HOP * far

        @pl.when(jnp.logical_and(m >= 0, m < msgs))
        def _():
            total[...] = own[m].astype(jnp.float32)

            @pl.when(row > 0)
            def _():
                total[...] += from_left[m].astype(jnp.float32)

            @pl.when(row < last_row)
            def _():
                total[...] += from_right[m].astype(jnp.float32)

        @pl.when(jnp.logical_and(m >= 0, m < steps))
        def _():
            value, slope_value = gelu_parts(total[...])
            slope[m] = slope_value
            block = value.astype(jnp.bfloat16)
            act_all[:, cols(m)] = block
            for n in range(0, d_model, TILE):
                acc_out[:, n : n + TILE] += jnp.dot(
                    block, w_out_v[m, :, n : n + TILE], preferred_element_type=jnp.float32
                )

        mo = m - steps

        @pl.when(jnp.logical_and(mo >= 0, mo < steps))
        def _():
            grad = (total[...] * slope[mo]).astype(jnp.bfloat16)
            hid_all[:, cols(mo)] = grad
            for n in range(0, d_model, TILE):
                acc_gin[:, n : n + TILE] += contract_cols(grad, w_in_v[mo, n : n + TILE, :])

        @pl.when(m == steps)
        def _():
            keep(2).start()
            send_pair(0, acc_out)

        @pl.when(m == steps + min(2, steps - 1))
        def _():
            send_parts(0, acc_out)

    keep(3).start()
    send_pair(1, acc_gin)
    send_parts(1, acc_gin)
    finish(0, out_ref)
    finish(1, gin_ref)

    for a in range(4):
        keep(a).wait()
    for a in range(2):
        for k in range(1, n_depth):
            depth_copy(a, k).wait_send()
            swap_copy(a, k).wait_send()
        for i in range(n_col // 2):
            pair_copy(a, i).wait_send()
        for k in range(1, group):
            part_copy(a, k).wait_send()

    @pl.loop(0, msgs)
    def _(m):
        @pl.when(row < last_row)
        def _():
            right_copy(m).wait_send()

        @pl.when(row > 0)
        def _():
            left_copy(m).wait_send()


def exchange(sizes, tokens, w_in, w_out, cotangent):
    n_row, n_col, n_depth = sizes
    slice_rows, d_model = tokens.shape
    rows = slice_rows * n_depth
    ff = w_in.shape[1]
    steps = ff // CHUNK
    msgs = 2 * steps
    group = (n_col // 2) * n_depth
    block_rows = rows // n_col
    piece_rows = block_rows // n_depth
    bf16, f32 = jnp.bfloat16, jnp.float32
    vmem = pl.BlockSpec(memory_space=pltpu.VMEM)
    hbm = pl.BlockSpec(memory_space=pl.ANY)
    dma = pltpu.SemaphoreType.DMA
    return pl.pallas_call(
        functools.partial(kernel, n_row, n_col, n_depth),
        out_shape=(
            jax.ShapeDtypeStruct((piece_rows, d_model), bf16),
            jax.ShapeDtypeStruct((piece_rows, d_model), bf16),
            jax.ShapeDtypeStruct((rows, d_model), bf16),
            jax.ShapeDtypeStruct((rows, d_model), bf16),
            jax.ShapeDtypeStruct((rows, ff), bf16),
            jax.ShapeDtypeStruct((rows, ff), bf16),
        ),
        in_specs=[vmem, hbm, hbm, vmem],
        out_specs=(vmem, vmem, hbm, hbm, hbm, hbm),
        scratch_shapes=[
            pltpu.VMEM((steps, d_model, CHUNK), bf16),
            pltpu.VMEM((steps, CHUNK, d_model), bf16),
            pltpu.VMEM((rows, d_model), bf16),
            pltpu.VMEM((rows, d_model), bf16),
            pltpu.VMEM((msgs, rows, CHUNK), bf16),
            pltpu.VMEM((msgs, rows, CHUNK), bf16),
            pltpu.VMEM((msgs, rows, CHUNK), bf16),
            pltpu.VMEM((msgs, rows, CHUNK), bf16),
            pltpu.VMEM((msgs, rows, CHUNK), bf16),
            pltpu.VMEM((rows, CHUNK), f32),
            pltpu.VMEM((steps, rows, CHUNK), f32),
            pltpu.VMEM((rows, ff), bf16),
            pltpu.VMEM((rows, ff), bf16),
            pltpu.VMEM((rows, d_model), f32),
            pltpu.VMEM((rows, d_model), f32),
            pltpu.VMEM((2, n_col // 2, block_rows, d_model), bf16),
            pltpu.VMEM((2, n_col // 2, block_rows, d_model), bf16),
            pltpu.VMEM((2, group, piece_rows, d_model), bf16),
            pltpu.VMEM((2, group - 1, piece_rows, d_model), bf16),
            dma((steps,)),
            dma((steps,)),
            dma((4,)),
            dma((2, msgs)),
            dma((2, msgs)),
            dma((2, 2, n_depth - 1)),
            dma((2, 2, n_depth - 1)),
            dma((2, 2, n_col // 2)),
            dma((2, 2, group - 1)),
        ],
        compiler_params=pltpu.CompilerParams(
            collective_id=0, has_side_effects=True, vmem_limit_bytes=62 * 2**20
        ),
        cost_estimate=pl.CostEstimate(
            flops=8 * rows * d_model * ff, bytes_accessed=4 * d_model * ff, transcendentals=rows * ff
        ),
        name="exchange",
    )(tokens, w_in, w_out, cotangent)


def body(sizes, tokens, w_in, w_out, cotangent):
    output, grad_input, all_tokens, all_grads, act, hidden = exchange(
        sizes, tokens, w_in, w_out, cotangent
    )
    grad_scale = all_tokens.shape[0] ** (-0.5)
    grad_w_out = (contract_rows(act, all_grads) * grad_scale).astype(jnp.bfloat16)
    grad_w_in = (contract_rows(all_tokens, hidden) * grad_scale).astype(jnp.bfloat16)
    return (output, grad_input, grad_w_in, grad_w_out)


def solution(mesh):
    sizes = (mesh.shape["row"], mesh.shape["col"], mesh.shape["depth"])
    in_specs = (
        P("depth", "row"),
        P("row", ("col", "depth")),
        P(("col", "depth"), "row"),
        P("depth", "row"),
    )
    out_specs = (
        P(("col", "depth"), "row"),
        P(("col", "depth"), "row"),
        P("row", ("col", "depth")),
        P(("col", "depth"), "row"),
    )
    return jax.shard_map(
        functools.partial(body, sizes),
        mesh=mesh,
        in_specs=in_specs,
        out_specs=out_specs,
        check_vma=False,
    )
```

time: 196 us -> 95.6 us (0.49)
  Pallas kernels: 0 us -> 73.1 us
  blocking collectives: 59.7 us -> 0 us
  matrix products: 66.1 us -> 20.4 us
  waiting for transfers between devices: 29.3 us -> 0 us
  local copies, waits for them, and re-layouts: 24.7 us -> 1.3 us
  between operations: 13.8 us -> 0.67 us
    pallas_call x0 -> x1, Pallas kernels: none -> 73.1 us  [exchange(): pl.pallas_call(functools.partial(kernel, n_row, n_col, n_depth), out_shap...]
    all_gather x4 -> x0, blocking collectives: 59.7 us -> none  [the longest x1 18 us: body(): lax.all_gather(gelu_value.astype(jnp.bfloat16), 'row', axis=0, tiled=True)]
    dot_general x4 -> x0, matrix products: 47.1 us -> none  [the longest x2 27.3 us: contract_cols(): lax.dot_general(left, right, (((1,), (1,)), ((), ())), preferred_element_...]
    reduce_scatter x4 -> x0, waiting for transfers between devices: 29.3 us -> none  [the longest x1 25.5 us: body(): lax.psum_scatter(jnp.dot(all_tokens, w_in, preferred_element_type=jnp.flo...]
    unnamed x3 -> x10, local copies, waits for them, and re-layouts: 24.7 us -> 1.3 us
  transfers between devices with their start and end apart: 4 -> 0, of which waited for: 2 -> 0; matrix products, arithmetic and copies ran while one was open for 35% -> 0% of each run, Pallas kernels for 0% -> 0%
where the time goes in v1:
time: 95.6 us; the launch traced here: 95.4 us
  Pallas kernels  73.1 us (76%)
  matrix products  20.4 us (21%)
  local copies, waits for them, and re-layouts  1.3 us (1%)
    pallas_call x1, Pallas kernels, exchange(): pl.pallas_call(functools.partial(kernel, n_row, n_col, n_depth), out_shap...  73.1 us
    dot_general x2, matrix products, contract_rows(): lax.dot_general(left, right, (((0,), (0,)), ((), ())), preferred_element_...  20.4 us

profile of v1, /device:TPU:0, one launch (start us, length us, event | category | flops | bytes accessed | tf_op | source)
XLA Modules:
  0.0 95.4 jit_solution(2782103524789684988)
XLA Ops:
  0.6 73.1 %exchange.1 = (bf16[16,3072]{1,0:T(8,128)(2,1)}, bf16[16,3072]{1,0:T(8,128)(2,1)}, bf16[128,3072]{1,0:T(8,128)(2,1)}, bf16[128,3072]{1,0:T(8,128)(2,1)}, bf16[12...) custom-call(bf16[64,3072]{1,0:T(8,128)(2,1)} %tok_ref.1, bf16[3072,3072]{1,0:T(8,128)(2,1)} %w_in_ref.1, ...), custom_call_target="tpu_custom_call" | custom-call | flops 9663676416 | bytes 37748736 | tf_op jit(solution)/shard_map/exchange/pallas_call | solution.py:419
  73.7 0.0 copy-start
  73.7 0.0 copy-start.1
  73.7 10.9 %multiply_convert_fusion.1 = bf16[3072,3072]{1,0:T(8,128)(2,1)} fusion(bf16[128,3072]{1,0:T(8,128)(2,1)} %get-tuple-element.12, bf16[128,3072]{1,0:T(8,128)(2,1)} %get-tuple-element.13), kind=kOutput, calls=%fused_computation.1 | convolution fusion | flops 2434793472 | bytes 20447232 | tf_op jit(solution)/shard_map/dot_general | solution.py:30
  84.6 0.0 copy-done
  84.6 0.0 copy-done.1
  84.6 0.0 copy-start.3
  84.6 0.0 copy-start.2
  84.6 9.5 %multiply_convert_fusion = bf16[3072,3072]{1,0:T(8,128)(2,1)} fusion(bf16[128,3072]{1,0:T(8,128)(2,1)S(1)} %copy-done, bf16[128,3072]{1,0:T(8,128)(2,1)S(1)} %copy-done.1), kind=kOutput, calls=%fused_computation | convolution fusion | flops 2434793472 | bytes 20447232 | tf_op jit(solution)/shard_map/dot_general | solution.py:30
  94.1 0.0 copy-done.3
  94.1 0.6 copy.10
  94.8 0.0 copy-done.2
  94.8 0.6 copy.11
Async XLA Ops:
  73.7 10.9 %copy-start = (bf16[128,3072]{1,0:T(8,128)(2,1)S(1)}, bf16[128,3072]{1,0:T(8,128)(2,1)}, u32[]{:S(2)}) copy-start(bf16[128,3072]{1,0:T(8,128)(2,1)} %get-tuple-element.14) | copy-start | bytes 2359300
  73.7 10.9 %copy-start.1 = (bf16[128,3072]{1,0:T(8,128)(2,1)S(1)}, bf16[128,3072]{1,0:T(8,128)(2,1)}, u32[]{:S(2)}) copy-start(bf16[128,3072]{1,0:T(8,128)(2,1)} %get-tuple-element.15) | copy-start | bytes 2359300
  84.6 9.5 %copy-start.3 = (bf16[16,3072]{1,0:T(8,128)(2,1)S(1)}, bf16[16,3072]{1,0:T(8,128)(2,1)}, u32[]{:S(2)}) copy-start(bf16[16,3072]{1,0:T(8,128)(2,1)} %get-tuple-element.20) | copy-start | bytes 294916
  84.6 10.2 %copy-start.2 = (bf16[16,3072]{1,0:T(8,128)(2,1)S(1)}, bf16[16,3072]{1,0:T(8,128)(2,1)}, u32[]{:S(2)}) copy-start(bf16[16,3072]{1,0:T(8,128)(2,1)} %get-tuple-element.21) | copy-start | bytes 294916

commit v2 on v1

--- a/solution.py
+++ b/solution.py
@@ -11,7 +11,8 @@
 MESH = pl.DeviceIdType.MESH
 CHUNK = 256
 TILE = 768
-HOP = 2
+HOP = 3
+GRAD_ROWS = 512
 
 gelu_coef = math.sqrt(2.0 / math.pi)
 
@@ -24,12 +25,6 @@
         1.0 + 3.0 * 0.044715 * preact * preact
     )
     return (gelu_value, gelu_slope)
-
-
-def contract_rows(left, right):
-    return lax.dot_general(
-        left, right, (((0,), (0,)), ((), ())), preferred_element_type=jnp.float32
-    )
 
 
 def contract_cols(left, right):
@@ -165,7 +160,7 @@
             device_id_type=MESH,
         )
 
-    for a in range(2):
+    def spread(a):
         for k in range(1, n_depth):
             depth_copy(a, k).start()
 
@@ -251,7 +246,9 @@
     def keep(a):
         return pltpu.make_async_copy(outs[a][0], outs[a][1], keep_sem.at[a])
 
+    spread(0)
     pass_on(0)
+    spread(1)
     arrived(0)
     keep(0).start()
 
@@ -468,13 +465,64 @@
     )(tokens, w_in, w_out, cotangent)
 
 
+def grads_kernel(scale, tok, hid, act, cot, out, gin, g_in, g_out, out_copy, gin_copy):
+    @pl.when(pl.program_id(0) == 0)
+    def _():
+        out_copy[...] = out[...]
+        gin_copy[...] = gin[...]
+
+    for left, right, result in ((tok, hid, g_in), (act, cot, g_out)):
+        turned = left[...].T
+        for n in range(0, right.shape[1], TILE):
+            result[:, n : n + TILE] = (
+                jnp.dot(turned, right[:, n : n + TILE], preferred_element_type=jnp.float32) * scale
+            ).astype(result.dtype)
+
+
+def weight_grads(tokens, hidden, act, grads, output, grad_input):
+    rows, d_model = tokens.shape
+    ff = hidden.shape[1]
+    bf16 = jnp.bfloat16
+    count = max(d_model, ff) // GRAD_ROWS
+    small = pl.BlockSpec(output.shape, lambda i: (0, 0))
+    return pl.pallas_call(
+        functools.partial(grads_kernel, rows ** (-0.5)),
+        grid=(count,),
+        out_shape=(
+            jax.ShapeDtypeStruct((d_model, ff), bf16),
+            jax.ShapeDtypeStruct((ff, d_model), bf16),
+            jax.ShapeDtypeStruct(output.shape, bf16),
+            jax.ShapeDtypeStruct(grad_input.shape, bf16),
+        ),
+        in_specs=[
+            pl.BlockSpec((rows, d_model // count), lambda i: (0, i)),
+            pl.BlockSpec((rows, ff), lambda i: (0, 0)),
+            pl.BlockSpec((rows, ff // count), lambda i: (0, i)),
+            pl.BlockSpec((rows, d_model), lambda i: (0, 0)),
+            small,
+            small,
+        ],
+        out_specs=(
+            pl.BlockSpec((d_model // count, ff), lambda i: (i, 0)),
+            pl.BlockSpec((ff // count, d_model), lambda i: (i, 0)),
+            small,
+            small,
+        ),
+        compiler_params=pltpu.CompilerParams(vmem_limit_bytes=62 * 2**20),
+        cost_estimate=pl.CostEstimate(
+            flops=4 * rows * d_model * ff, bytes_accessed=4 * d_model * ff, transcendentals=0
+        ),
+        name="weight_grads",
+    )(tokens, hidden, act, grads, output, grad_input)
+
+
 def body(sizes, tokens, w_in, w_out, cotangent):
     output, grad_input, all_tokens, all_grads, act, hidden = exchange(
         sizes, tokens, w_in, w_out, cotangent
     )
-    grad_scale = all_tokens.shape[0] ** (-0.5)
-    grad_w_out = (contract_rows(act, all_grads) * grad_scale).astype(jnp.bfloat16)
-    grad_w_in = (contract_rows(all_tokens, hidden) * grad_scale).astype(jnp.bfloat16)
+    grad_w_in, grad_w_out, output, grad_input = weight_grads(
+        all_tokens, hidden, act, all_grads, output, grad_input
+    )
     return (output, grad_input, grad_w_in, grad_w_out)
 
 

time: 95.6 us -> 82.9 us (0.87)
  matrix products: 20.4 us -> 0 us
  Pallas kernels: 73.1 us -> 82 us
  local copies, waits for them, and re-layouts: 1.3 us -> 0 us
    dot_general x2 -> x0, matrix products: 20.4 us -> none  [contract_rows(): lax.dot_general(left, right, (((0,), (0,)), ((), ())), preferred_element_...]
    pallas_call x0 -> x1, Pallas kernels: none -> 14.9 us  [weight_grads(): pl.pallas_call(functools.partial(grads_kernel, rows ** (-0.5)), grid=(cou...]
    pallas_call x1, Pallas kernels: 73.1 us -> 67.2 us  [exchange(): pl.pallas_call(functools.partial(kernel, n_row, n_col, n_depth), out_shap...]
    unnamed x10 -> x0, local copies, waits for them, and re-layouts: 1.3 us -> none
where the time goes in v2:
time: 82.9 us; the launch traced here: 82.7 us
  Pallas kernels  82 us (99%)
    pallas_call x1, Pallas kernels, exchange(): pl.pallas_call(functools.partial(kernel, n_row, n_col, n_depth), out_shap...  67.2 us
    pallas_call x1, Pallas kernels, weight_grads(): pl.pallas_call(functools.partial(grads_kernel, rows ** (-0.5)), grid=(cou...  14.9 us

profile of v2, /device:TPU:0, one launch (start us, length us, event | category | flops | bytes accessed | tf_op | source)
XLA Modules:
  0.0 82.7 jit_solution(13119862316633246514)
XLA Ops:
  0.6 67.2 %exchange.1 = (bf16[16,3072]{1,0:T(8,128)(2,1)}, bf16[16,3072]{1,0:T(8,128)(2,1)}, bf16[128,3072]{1,0:T(8,128)(2,1)}, bf16[128,3072]{1,0:T(8,128)(2,1)}, bf16[12...) custom-call(bf16[64,3072]{1,0:T(8,128)(2,1)} %tok_ref.1, bf16[3072,3072]{1,0:T(8,128)(2,1)} %w_in_ref.1, ...), custom_call_target="tpu_custom_call" | custom-call | flops 9663676416 | bytes 37748736 | tf_op jit(solution)/shard_map/exchange/pallas_call | solution.py:416
  67.8 14.9 %weight_grads.1 = (bf16[3072,3072]{1,0:T(8,128)(2,1)}, bf16[3072,3072]{1,0:T(8,128)(2,1)}, bf16[16,3072]{1,0:T(8,128)(2,1)}, bf16[16,3072]{1,0:T(8,128)(2,1)}) custom-call(bf16[128,3072]{1,0:T(8,128)(2,1)} %get-tuple-element.14.tok, bf16[128,3072]{1,0:T(8,128)(2,1)} %get-tuple-element.15.hid, bf16[128,3072]{1,0:T(8,128)(2,1)} %get-tuple-element.16.act, ...), custom_call_target="tpu_custom_call" | custom-call | flops 4831838208 | bytes 37748736 | tf_op jit(solution)/shard_map/weight_grads/pallas_call | solution.py:488

commit v3 on v2

--- a/solution.py
+++ b/solution.py
@@ -373,8 +373,8 @@
 
     keep(3).start()
     send_pair(1, acc_gin)
+    finish(0, out_ref)
     send_parts(1, acc_gin)
-    finish(0, out_ref)
     finish(1, gin_ref)
 
     for a in range(4):

time: 82.9 us -> 82.9 us (level)
  no operation moved by 1% of the time
where the time goes in v3:
time: 82.9 us; the launch traced here: 82.7 us
  Pallas kernels  82 us (99%)
    pallas_call x1, Pallas kernels, exchange(): pl.pallas_call(functools.partial(kernel, n_row, n_col, n_depth), out_shap...  67.2 us
    pallas_call x1, Pallas kernels, weight_grads(): pl.pallas_call(functools.partial(grads_kernel, rows ** (-0.5)), grid=(cou...  14.9 us

profile of v3, /device:TPU:0, one launch (start us, length us, event | category | flops | bytes accessed | tf_op | source)
XLA Modules:
  0.0 82.7 jit_solution(18385338241898592995)
XLA Ops:
  0.6 67.2 %exchange.1 = (bf16[16,3072]{1,0:T(8,128)(2,1)}, bf16[16,3072]{1,0:T(8,128)(2,1)}, bf16[128,3072]{1,0:T(8,128)(2,1)}, bf16[128,3072]{1,0:T(8,128)(2,1)}, bf16[12...) custom-call(bf16[64,3072]{1,0:T(8,128)(2,1)} %tok_ref.1, bf16[3072,3072]{1,0:T(8,128)(2,1)} %w_in_ref.1, ...), custom_call_target="tpu_custom_call" | custom-call | flops 9663676416 | bytes 37748736 | tf_op jit(solution)/shard_map/exchange/pallas_call | solution.py:416
  67.8 14.9 %weight_grads.1 = (bf16[3072,3072]{1,0:T(8,128)(2,1)}, bf16[3072,3072]{1,0:T(8,128)(2,1)}, bf16[16,3072]{1,0:T(8,128)(2,1)}, bf16[16,3072]{1,0:T(8,128)(2,1)}) custom-call(bf16[128,3072]{1,0:T(8,128)(2,1)} %get-tuple-element.14.tok, bf16[128,3072]{1,0:T(8,128)(2,1)} %get-tuple-element.15.hid, bf16[128,3072]{1,0:T(8,128)(2,1)} %get-tuple-element.16.act, ...), custom_call_target="tpu_custom_call" | custom-call | flops 4831838208 | bytes 37748736 | tf_op jit(solution)/shard_map/weight_grads/pallas_call | solution.py:488
